TPU v7x, 512 devices: a whole 4x8x8 slice. The times are simulated.
512 devices in a mesh: seq: 128 (over z_lo, x, y, core), head: 4 (over z_hi).
Axes of the slice: x: 4, y: 8, z: 8 (z_hi: 4, z_lo: 2; z = z_hi * 2 + z_lo), core: 2. Of those that a mesh axis runs over, the one named last changes fastest.
Arguments:
- queries: bfloat16 [16384, 4096], P('seq', 'head'), may hold values from -6 to 6
- key_rows: bfloat16 [16384, 4096], P('seq', 'head'), may hold values from -6 to 6
- values: bfloat16 [16384, 4096], P('seq', 'head'), may hold values from -11 to 11
- out_grad: bfloat16 [16384, 4096], P('seq', 'head'), may hold values from -11 to 11
- norm_gain: float32 [4096], P('head'), may hold values from 0.1 to 1.9
- head_levels: int32 [32, 7], P('head'), may hold values 0 or 1
Outputs:
- normed: bfloat16 [16384, 4096], P('seq', 'head')
- query_grad: bfloat16 [16384, 4096], P('seq', 'head')
- key_grad: bfloat16 [16384, 4096], P('seq', 'head')
- value_grad: bfloat16 [16384, 4096], P('seq', 'head')
- gain_grad: float32 [4096], P('head')
Inputs may be any that keep to these rules, and one draw needn't show every extreme that they name: head_levels[h, l] is 1 where head h reads the block 2**l blocks back.
All inputs are finite; a program needn't handle non-finite values.
Results may differ from a plain program's by a relative error of at most 0.018.
Values may be sent and summed in bfloat16 or wider, within the bound.
A program may use at most 64 MiB of HBM per device.

v0:
```python
import math

import jax
import jax.numpy as jnp
from jax import lax
from jax.sharding import PartitionSpec as P

D = 4096
HEAD_DIM = 128


EPSILON = 1e-06


def shifted(x, axis, by):
    devices = lax.axis_size(axis)
    pairs = [(i, i + by) for i in range(devices) if 0 <= i + by < devices]
    return lax.ppermute(x, axis, pairs)


def column_block(matrix, which_head, head_size):
    return lax.dynamic_slice_in_dim(matrix, which_head * head_size, head_size, 1)


def place_cols(buffer, portion, which_head, head_size):
    return lax.dynamic_update_slice_in_dim(buffer, portion, which_head * head_size, 1)


def contract_cols(left_side, right_side):
    return lax.dot_general(
        left_side, right_side, (((1,), (1,)), ((), ())), preferred_element_type=jnp.float32
    )


def contract_rows(left_side, right_side):
    return lax.dot_general(
        left_side, right_side, (((0,), (0,)), ((), ())), preferred_element_type=jnp.float32
    )


def body(queries, key_rows, values, out_grad, norm_gain, head_levels):
    f32 = jnp.float32
    bf16 = jnp.bfloat16
    tok_rows, row_width = queries.shape
    head_size = HEAD_DIM
    local_heads = row_width // head_size
    seq_devices = lax.axis_size("seq")
    level_count = seq_devices.bit_length() - 1
    block_index = lax.axis_index("seq")
    score_scale = 1.0 / math.sqrt(head_size)
    fetched = []
    for exponent in range(level_count):
        fetched.append(shifted((key_rows, values), "seq", 2**exponent))
    near_keys = jnp.concatenate([key_rows] + [received[0] for received in fetched], axis=0)
    near_values = jnp.concatenate([values] + [received[1] for received in fetched], axis=0)
    key_count = near_keys.shape[0]
    distance = 2 ** jnp.arange(level_count, dtype=jnp.int32)
    level_live = (head_levels == 1) & (block_index >= distance)[None, :]
    block_live = jnp.concatenate([jnp.ones((local_heads, 1), jnp.bool_), level_live], axis=1)
    key_block = jnp.arange(key_count, dtype=jnp.int32) // tok_rows
    key_place = jnp.arange(key_count, dtype=jnp.int32) % tok_rows
    row_place = jnp.arange(tok_rows, dtype=jnp.int32)
    causal = (key_block[None, :] > 0) | (key_place[None, :] <= row_place[:, None])
    block_hit = key_block[None, :] == jnp.arange(level_count + 1, dtype=jnp.int32)[:, None]

    def forward_head(which_head, buffers):
        context, weight_store, max_store, sum_store = buffers
        query_head = column_block(queries, which_head, head_size)
        key_head = column_block(near_keys, which_head, head_size)
        value_head = column_block(near_values, which_head, head_size)
        live_keys = jnp.any(block_hit & block_live[which_head][:, None], axis=0)
        scores = contract_cols(query_head, key_head) * score_scale
        scores = jnp.where(causal & live_keys[None, :], scores, -jnp.inf)
        row_max = jnp.max(scores, axis=1)
        raw_weights = jnp.exp(scores - row_max[:, None])
        row_sum = jnp.sum(raw_weights, axis=1)
        weights = (raw_weights / row_sum[:, None]).astype(bf16)
        head_out = jnp.dot(weights, value_head, preferred_element_type=f32).astype(bf16)
        return (
            place_cols(context, head_out, which_head, head_size),
            weight_store.at[which_head].set(weights),
            max_store.at[which_head].set(row_max),
            sum_store.at[which_head].set(row_sum),
        )

    start_buffers = (
        jnp.zeros((tok_rows, row_width), bf16),
        jnp.zeros((local_heads, tok_rows, key_count), bf16),
        jnp.zeros((local_heads, tok_rows), f32),
        jnp.zeros((local_heads, tok_rows), f32),
    )
    context, weight_store, max_store, sum_store = lax.fori_loop(
        0, local_heads, forward_head, start_buffers
    )
    context_f = context.astype(f32)
    squares = lax.psum(jnp.sum(context_f * context_f, axis=1), "head")
    inverse = lax.rsqrt(squares / D + EPSILON)
    normed = (context_f * inverse[:, None] * norm_gain[None, :]).astype(bf16)
    out_f = out_grad.astype(f32)
    scaled_grad = norm_gain[None, :] * out_f
    correction = lax.psum(jnp.sum(scaled_grad * context_f, axis=1), "head")
    context_grad = (
        inverse[:, None] * scaled_grad
        - (inverse * inverse * inverse * correction / D)[:, None] * context_f
    ).astype(bf16)
    gain_local = jnp.sum(out_f * context_f * inverse[:, None], axis=0)
    gain_grad = lax.psum(gain_local, "seq") / math.sqrt(seq_devices * tok_rows)
    out_dots = jnp.sum(
        (context_grad.astype(f32) * context_f).reshape(tok_rows, local_heads, head_size), axis=2
    ).T
    far_rows = key_count - tok_rows

    def backward_head(which_head, buffers):
        query_grad, key_near, value_near, key_far, value_far = buffers
        query_head = column_block(queries, which_head, head_size)
        key_head = column_block(near_keys, which_head, head_size)
        value_head = column_block(near_values, which_head, head_size)
        grad_head = column_block(context_grad, which_head, head_size)
        weights = weight_store[which_head]
        weight_grad = contract_cols(grad_head, value_head)
        score_grad = (
            weights.astype(f32) * (weight_grad - out_dots[which_head][:, None]) * score_scale
        ).astype(bf16)
        query_grad = place_cols(
            query_grad,
            jnp.dot(score_grad, key_head, preferred_element_type=f32).astype(bf16),
            which_head,
            head_size,
        )
        key_terms = contract_rows(score_grad, query_head)
        value_terms = contract_rows(weights, grad_head)
        key_near = place_cols(key_near, key_terms[:tok_rows], which_head, head_size)
        value_near = place_cols(value_near, value_terms[:tok_rows], which_head, head_size)
        key_far = place_cols(key_far, key_terms[tok_rows:].astype(bf16), which_head, head_size)
        value_far = place_cols(
            value_far, value_terms[tok_rows:].astype(bf16), which_head, head_size
        )
        return (query_grad, key_near, value_near, key_far, value_far)

    start_grads = (
        jnp.zeros((tok_rows, row_width), bf16),
        jnp.zeros((tok_rows, row_width), f32),
        jnp.zeros((tok_rows, row_width), f32),
        jnp.zeros((far_rows, row_width), bf16),
        jnp.zeros((far_rows, row_width), bf16),
    )
    query_grad, key_total, value_total, key_far, value_far = lax.fori_loop(
        0, local_heads, backward_head, start_grads
    )
    for exponent in range(level_count):
        first_row = exponent * tok_rows
        back_keys, back_values = shifted(
            (
                key_far[first_row : first_row + tok_rows],
                value_far[first_row : first_row + tok_rows],
            ),
            "seq",
            -(2**exponent),
        )
        key_total = key_total + back_keys.astype(f32)
        value_total = value_total + back_values.astype(f32)
    return (normed, query_grad, key_total.astype(bf16), value_total.astype(bf16), gain_grad)


def solution(mesh):
    placed = (
        P("seq", "head"),
        P("seq", "head"),
        P("seq", "head"),
        P("seq", "head"),
        P("head"),
        P("head", None),
    )
    return jax.shard_map(
        body,
        mesh=mesh,
        in_specs=placed,
        out_specs=(
            P("seq", "head"),
            P("seq", "head"),
            P("seq", "head"),
            P("seq", "head"),
            P("head"),
        ),
        check_vma=False,
    )
```

profile of v0, /device:TPU:74, one launch (start us, length us, event | category | flops | bytes accessed | tf_op | source)
XLA Modules:
  0.0 562.1 jit_solution(15485828811725810289)
XLA Ops:
  0.6 4.2 collective-permute-start.5
  6.7 4.5 collective-permute-start.2
  11.3 4.7 collective-permute-start.1
  16.0 1.9 collective-permute-start
  21.3 10.5 %collective-permute-done = bf16[128,1024]{1,0:T(8,128)(2,1)} collective-permute-done((bf16[128,1024]{1,0:T(8,128)(2,1)}, bf16[128,1024]{1,0:T(8,128)(2,1)}, u32[]{:S(2)}, u32[]{:S(2)}) %collective-permute-start) | collective-permute-done | bytes 262176 | tf_op jit(solution)/shard_map/ppermute | solution.py:18
  31.9 5.9 %collective-permute-start.3 = (bf16[128,1024]{1,0:T(8,128)(2,1)}, bf16[128,1024]{1,0:T(8,128)(2,1)S(1)}, u32[]{:S(2)}, u32[]{:S(2)}) collective-permute-start(bf16[128,1024]{1,0:T(8,128)(2,1)} %param.13), channel_id=1, source_target_pairs={{0,32},{4,36},{8,40},{12,44},{16,48},{20,52},{24,56},{28,60},{32,6... | collective-permute-start | bytes 786440 | tf_op jit(solution)/shard_map/ppermute | solution.py:18
  44.2 7.2 %collective-permute-done.3 = bf16[128,1024]{1,0:T(8,128)(2,1)S(1)} collective-permute-done((bf16[128,1024]{1,0:T(8,128)(2,1)}, bf16[128,1024]{1,0:T(8,128)(2,1)S(1)}, u32[]{:S(2)}, u32[]{:S(2)}) %collective-permute-start.3) | collective-permute-done | bytes 262176 | tf_op jit(solution)/shard_map/ppermute | solution.py:18
  51.4 2.3 collective-permute-start.11
  57.0 4.3 collective-permute-start.8
  62.1 3.2 collective-permute-start.9
  66.0 2.7 collective-permute-start.10
  70.5 22.1 %collective-permute-done.9 = bf16[128,1024]{1,0:T(8,128)(2,1)S(1)} collective-permute-done((bf16[128,1024]{1,0:T(8,128)(2,1)S(1)}, bf16[128,1024]{1,0:T(8,128)(2,1)S(1)}, u32[]{:S(2)}, u32[]{:S(2)}) %collective-permute-start.9) | collective-permute-done | bytes 262176 | tf_op jit(solution)/shard_map/ppermute | solution.py:18
  94.4 36.2 %while.39 = (s32[]{:T(128)}, bf16[128,1024]{1,0:T(8,128)(2,1)S(1)}, bf16[8,128,1024]{2,1,0:T(8,128)(2,1)S(1)}, pred[8,8]{1,0:T(8,128)(4,1)S(1)}, bf16[128,1024]{...) while((s32[]{:T(128)}, bf16[128,1024]{1,0:T(8,128)(2,1)S(1)}, ...), condition=%wide.region_5.6_spmd.clone, body=%wide.region_0.5_spmd.clone.sunk | while | flops 69114640 | bytes 3228417 | solution.py:92
  130.7 18.2 %psum.21 = f32[128]{0:T(128)S(1)} all-reduce(f32[128]{0:T(128)S(1)} %fusion.40), channel_id=1, replica_groups=mesh['seq'=128,'head'=4] {'head'}, use_global_device_ids=true, to_apply=%region_7.8 | all-reduce | flops 128 | bytes 1024 | tf_op jit(solution)/shard_map/psum | solution.py:96
  149.2 9.2 %psum.22 = f32[128]{0:T(128)S(1)} all-reduce(f32[128]{0:T(128)S(1)} %get-tuple-element.443), channel_id=1, replica_groups=mesh['seq'=128,'head'=4] {'head'}, use_global_device_ids=true, to_apply=%region_9.10 | all-reduce | flops 128 | bytes 1024 | tf_op jit(solution)/shard_map/psum | solution.py:101
  163.5 41.5 %while.38 = (s32[]{:T(128)}, bf16[128,1024]{1,0:T(8,128)(2,1)}, f32[128,1024]{1,0:T(8,128)S(1)}, f32[128,1024]{1,0:T(8,128)S(1)}, bf16[896,1024]{1,0:T(8,128)(2,...) while((s32[]{:T(128)}, bf16[128,1024]{1,0:T(8,128)(2,1)}, ...), condition=%wide.region_12.13_spmd, body=%wide.region_11.12_spmd.sunk | while | flops 134889472 | bytes 4198627 | solution.py:147
  208.6 3.1 collective-permute-start.27
  211.7 7.1 %collective-permute-start.26 = (bf16[128,1024]{1,0:T(8,128)(2,1)S(1)}, bf16[128,1024]{1,0:T(8,128)(2,1)S(1)}, u32[]{:S(2)}, u32[]{:S(2)}) collective-permute-start(bf16[128,1024]{1,0:T(8,128)(2,1)S(1)} %get-tuple-element.498), channel_id=1, source_target_pairs={{128,0},{132,4},{136,8},{140,12},{144,16},{148,20},{152,24},{156,2... | collective-permute-start | bytes 786440 | tf_op jit(solution)/shard_map/ppermute | solution.py:18
  218.8 2.0 collective-permute-start.25
  223.7 5.8 %collective-permute-start.23 = (bf16[128,1024]{1,0:T(8,128)(2,1)S(1)}, bf16[128,1024]{1,0:T(8,128)(2,1)}, u32[]{:S(2)}, u32[]{:S(2)}) collective-permute-start(bf16[128,1024]{1,0:T(8,128)(2,1)S(1)} %get-tuple-element.501), channel_id=1, source_target_pairs={{16,0},{20,4},{24,8},{28,12},{32,16},{36,20},{40,24},{44,28},{48,3... | collective-permute-start | bytes 786440 | tf_op jit(solution)/shard_map/ppermute | solution.py:18
  229.5 3.3 collective-permute-start.22
  232.8 3.2 collective-permute-start.14
  236.0 2.0 collective-permute-start.20
  238.1 242.7 %psum.23 = f32[1024]{0:T(1024)S(1)} all-reduce(f32[1024]{0:T(1024)S(1)} %get-tuple-element.442), channel_id=1, replica_groups=mesh['seq'=128,'head'=4] {'seq'}, use_global_device_ids=true, to_apply=%region_14.15 | all-reduce | flops 1024 | bytes 8192 | tf_op jit(solution)/shard_map/psum | solution.py:107
  481.3 11.6 %collective-permute-start.19 = (bf16[128,1024]{1,0:T(8,128)(2,1)S(1)}, bf16[128,1024]{1,0:T(8,128)(2,1)S(1)}, u32[]{:S(2)}, u32[]{:S(2)}) collective-permute-start(bf16[128,1024]{1,0:T(8,128)(2,1)S(1)} %get-tuple-element.505), channel_id=1, source_target_pairs={{128,0},{132,4},{136,8},{140,12},{144,16},{148,20},{152,24},{156,2... | collective-permute-start | bytes 786440 | tf_op jit(solution)/shard_map/ppermute | solution.py:18
  493.0 35.4 %collective-permute-start.18 = (bf16[128,1024]{1,0:T(8,128)(2,1)S(1)}, bf16[128,1024]{1,0:T(8,128)(2,1)S(1)}, u32[]{:S(2)}, u32[]{:S(2)}) collective-permute-start(bf16[128,1024]{1,0:T(8,128)(2,1)S(1)} %get-tuple-element.506), channel_id=1, source_target_pairs={{64,0},{68,4},{72,8},{76,12},{80,16},{84,20},{88,24},{92,28},{96,3... | collective-permute-start | bytes 786440 | tf_op jit(solution)/shard_map/ppermute | solution.py:18
  530.3 3.4 collective-permute-start.16
  533.7 6.9 %collective-permute-start.15 = (bf16[128,1024]{1,0:T(8,128)(2,1)S(1)}, bf16[128,1024]{1,0:T(8,128)(2,1)S(1)}, u32[]{:S(2)}, u32[]{:S(2)}) collective-permute-start(bf16[128,1024]{1,0:T(8,128)(2,1)S(1)} %get-tuple-element.509), channel_id=1, source_target_pairs={{8,0},{12,4},{16,8},{20,12},{24,16},{28,20},{32,24},{36,28},{40,32... | collective-permute-start | bytes 786440 | tf_op jit(solution)/shard_map/ppermute | solution.py:18
  540.7 2.5 add_convert_fusion
  543.4 6.4 %collective-permute-done.16 = bf16[128,1024]{1,0:T(8,128)(2,1)S(1)} collective-permute-done((bf16[128,1024]{1,0:T(8,128)(2,1)S(1)}, bf16[128,1024]{1,0:T(8,128)(2,1)S(1)}, u32[]{:S(2)}, u32[]{:S(2)}) %collective-permute-start.16) | collective-permute-done | bytes 262176 | tf_op jit(solution)/shard_map/ppermute | solution.py:18
  549.8 10.3 %collective-permute-done.15 = bf16[128,1024]{1,0:T(8,128)(2,1)S(1)} collective-permute-done((bf16[128,1024]{1,0:T(8,128)(2,1)S(1)}, bf16[128,1024]{1,0:T(8,128)(2,1)S(1)}, u32[]{:S(2)}, u32[]{:S(2)}) %collective-permute-start.15) | collective-permute-done | bytes 262176 | tf_op jit(solution)/shard_map/ppermute | solution.py:18
  560.1 2.1 add_convert_fusion.1
  (202 shorter events, 111.9 us)
Async XLA Ops:
  0.6 40.9 %copy-start.7 = (bf16[128,1024]{1,0:T(8,128)(2,1)S(1)}, bf16[128,1024]{1,0:T(8,128)(2,1)}, u32[]{:S(2)}) copy-start(bf16[128,1024]{1,0:T(8,128)(2,1)} %param.14) | copy-start | bytes 786436
  0.6 56.4 %collective-permute-start.5 = (bf16[128,1024]{1,0:T(8,128)(2,1)}, bf16[128,1024]{1,0:T(8,128)(2,1)S(1)}, u32[]{:S(2)}, u32[]{:S(2)}) collective-permute-start(bf16[128,1024]{1,0:T(8,128)(2,1)} %param.13), channel_id=1, source_target_pairs={{0,128},{4,132},{8,136},{12,140},{16,144},{20,148},{24,152},{28,15... | collective-permute-start | bytes 786440 | tf_op jit(solution)/shard_map/ppermute | solution.py:18
  4.8 49.5 %collective-permute-start.4 = (bf16[128,1024]{1,0:T(8,128)(2,1)}, bf16[128,1024]{1,0:T(8,128)(2,1)S(1)}, u32[]{:S(2)}, u32[]{:S(2)}) collective-permute-start(bf16[128,1024]{1,0:T(8,128)(2,1)} %param.13), channel_id=1, source_target_pairs={{0,64},{4,68},{8,72},{12,76},{16,80},{20,84},{24,88},{28,92},{32,9... | collective-permute-start | bytes 786440 | tf_op jit(solution)/shard_map/ppermute | solution.py:18
  6.7 34.8 %collective-permute-start.2 = (bf16[128,1024]{1,0:T(8,128)(2,1)}, bf16[128,1024]{1,0:T(8,128)(2,1)S(1)}, u32[]{:S(2)}, u32[]{:S(2)}) collective-permute-start(bf16[128,1024]{1,0:T(8,128)(2,1)} %param.13), channel_id=1, source_target_pairs={{0,16},{4,20},{8,24},{12,28},{16,32},{20,36},{24,40},{28,44},{32,4... | collective-permute-start | bytes 786440 | tf_op jit(solution)/shard_map/ppermute | solution.py:18
  11.3 28.2 %collective-permute-start.1 = (bf16[128,1024]{1,0:T(8,128)(2,1)}, bf16[128,1024]{1,0:T(8,128)(2,1)S(1)}, u32[]{:S(2)}, u32[]{:S(2)}) collective-permute-start(bf16[128,1024]{1,0:T(8,128)(2,1)} %param.13), channel_id=1, source_target_pairs={{0,8},{4,12},{8,16},{12,20},{16,24},{20,28},{24,32},{28,36},{32,40... | collective-permute-start | bytes 786440 | tf_op jit(solution)/shard_map/ppermute | solution.py:18
  16.0 15.9 %collective-permute-start = (bf16[128,1024]{1,0:T(8,128)(2,1)}, bf16[128,1024]{1,0:T(8,128)(2,1)}, u32[]{:S(2)}, u32[]{:S(2)}) collective-permute-start(bf16[128,1024]{1,0:T(8,128)(2,1)} %param.13), channel_id=1, source_target_pairs={{0,4},{4,8},{8,12},{12,16},{16,20},{20,24},{24,28},{28,32},{32,36}... | collective-permute-start | bytes 786440 | tf_op jit(solution)/shard_map/ppermute | solution.py:18
  31.9 19.5 %collective-permute-start.3 = (bf16[128,1024]{1,0:T(8,128)(2,1)}, bf16[128,1024]{1,0:T(8,128)(2,1)S(1)}, u32[]{:S(2)}, u32[]{:S(2)}) collective-permute-start(bf16[128,1024]{1,0:T(8,128)(2,1)} %param.13), channel_id=1, source_target_pairs={{0,32},{4,36},{8,40},{12,44},{16,48},{20,52},{24,56},{28,60},{32,6... | collective-permute-start | bytes 786440 | tf_op jit(solution)/shard_map/ppermute | solution.py:18
  39.5 22.6 %collective-permute-start.6 = (bf16[128,1024]{1,0:T(8,128)(2,1)}, bf16[128,1024]{1,0:T(8,128)(2,1)S(1)}, u32[]{:S(2)}, u32[]{:S(2)}) collective-permute-start(bf16[128,1024]{1,0:T(8,128)(2,1)} %param.13), channel_id=1, source_target_pairs={{0,256},{4,260},{8,264},{12,268},{16,272},{20,276},{24,280},{28,28... | collective-permute-start | bytes 786440 | tf_op jit(solution)/shard_map/ppermute | solution.py:18
  41.5 51.2 %collective-permute-start.12 = (bf16[128,1024]{1,0:T(8,128)(2,1)S(1)}, bf16[128,1024]{1,0:T(8,128)(2,1)S(1)}, u32[]{:S(2)}, u32[]{:S(2)}) collective-permute-start(bf16[128,1024]{1,0:T(8,128)(2,1)S(1)} %copy-done.7), channel_id=1, source_target_pairs={{0,128},{4,132},{8,136},{12,140},{16,144},{20,148},{24,152},{28,15... | collective-permute-start | bytes 786440 | tf_op jit(solution)/shard_map/ppermute | solution.py:18
  51.4 41.3 %collective-permute-start.11 = (bf16[128,1024]{1,0:T(8,128)(2,1)S(1)}, bf16[128,1024]{1,0:T(8,128)(2,1)S(1)}, u32[]{:S(2)}, u32[]{:S(2)}) collective-permute-start(bf16[128,1024]{1,0:T(8,128)(2,1)S(1)} %copy-done.7), channel_id=1, source_target_pairs={{0,64},{4,68},{8,72},{12,76},{16,80},{20,84},{24,88},{28,92},{32,9... | collective-permute-start | bytes 786440 | tf_op jit(solution)/shard_map/ppermute | solution.py:18
  54.4 11.6 %collective-permute-start.7 = (bf16[128,1024]{1,0:T(8,128)(2,1)S(1)}, bf16[128,1024]{1,0:T(8,128)(2,1)S(1)}, u32[]{:S(2)}, u32[]{:S(2)}) collective-permute-start(bf16[128,1024]{1,0:T(8,128)(2,1)S(1)} %copy-done.7), channel_id=1, source_target_pairs={{0,4},{4,8},{8,12},{12,16},{16,20},{20,24},{24,28},{28,32},{32,36}... | collective-permute-start | bytes 786440 | tf_op jit(solution)/shard_map/ppermute | solution.py:18
  57.0 12.2 %collective-permute-start.8 = (bf16[128,1024]{1,0:T(8,128)(2,1)S(1)}, bf16[128,1024]{1,0:T(8,128)(2,1)S(1)}, u32[]{:S(2)}, u32[]{:S(2)}) collective-permute-start(bf16[128,1024]{1,0:T(8,128)(2,1)S(1)} %copy-done.7), channel_id=1, source_target_pairs={{0,8},{4,12},{8,16},{12,20},{16,24},{20,28},{24,32},{28,36},{32,40... | collective-permute-start | bytes 786440 | tf_op jit(solution)/shard_map/ppermute | solution.py:18
  62.1 30.5 %collective-permute-start.9 = (bf16[128,1024]{1,0:T(8,128)(2,1)S(1)}, bf16[128,1024]{1,0:T(8,128)(2,1)S(1)}, u32[]{:S(2)}, u32[]{:S(2)}) collective-permute-start(bf16[128,1024]{1,0:T(8,128)(2,1)S(1)} %copy-done.7), channel_id=1, source_target_pairs={{0,16},{4,20},{8,24},{12,28},{16,32},{20,36},{24,40},{28,44},{32,4... | collective-permute-start | bytes 786440 | tf_op jit(solution)/shard_map/ppermute | solution.py:18
  66.0 26.6 %collective-permute-start.10 = (bf16[128,1024]{1,0:T(8,128)(2,1)S(1)}, bf16[128,1024]{1,0:T(8,128)(2,1)S(1)}, u32[]{:S(2)}, u32[]{:S(2)}) collective-permute-start(bf16[128,1024]{1,0:T(8,128)(2,1)S(1)} %copy-done.7), channel_id=1, source_target_pairs={{0,32},{4,36},{8,40},{12,44},{16,48},{20,52},{24,56},{28,60},{32,6... | collective-permute-start | bytes 786440 | tf_op jit(solution)/shard_map/ppermute | solution.py:18
  69.2 23.6 %collective-permute-start.13 = (bf16[128,1024]{1,0:T(8,128)(2,1)S(1)}, bf16[128,1024]{1,0:T(8,128)(2,1)S(1)}, u32[]{:S(2)}, u32[]{:S(2)}) collective-permute-start(bf16[128,1024]{1,0:T(8,128)(2,1)S(1)} %copy-done.7), channel_id=1, source_target_pairs={{0,256},{4,260},{8,264},{12,268},{16,272},{20,276},{24,280},{28,28... | collective-permute-start | bytes 786440 | tf_op jit(solution)/shard_map/ppermute | solution.py:18
  94.4 54.6 %copy-start.2 = (bf16[128,1024]{1,0:T(8,128)(2,1)S(1)}, bf16[128,1024]{1,0:T(8,128)(2,1)}, u32[]{:S(2)}) copy-start(bf16[128,1024]{1,0:T(8,128)(2,1)} %param.15) | copy-start | bytes 786436
  94.4 54.6 %copy-start.8 = (f32[1024]{0:T(1024)S(1)}, f32[1024]{0:T(1024)}, u32[]{:S(2)}) copy-start(f32[1024]{0:T(1024)} %param.16) | copy-start | bytes 12292
  205.0 17.8 %copy-start = (bf16[896,1024]{1,0:T(8,128)(2,1)S(1)}, bf16[896,1024]{1,0:T(8,128)(2,1)}, u32[]{:S(2)}) copy-start(bf16[896,1024]{1,0:T(8,128)(2,1)} %get-tuple-element.389) | copy-start | bytes 5505028
  206.7 17.0 %collective-permute-start.21 = (bf16[128,1024]{1,0:T(8,128)(2,1)S(1)}, bf16[128,1024]{1,0:T(8,128)(2,1)S(1)}, u32[]{:S(2)}, u32[]{:S(2)}) collective-permute-start(bf16[128,1024]{1,0:T(8,128)(2,1)S(1)} %get-tuple-element.496), channel_id=1, source_target_pairs={{4,0},{8,4},{12,8},{16,12},{20,16},{24,20},{28,24},{32,28},{36,32}... | collective-permute-start | bytes 786440 | tf_op jit(solution)/shard_map/ppermute | solution.py:18
  208.6 20.9 %collective-permute-start.27 = (bf16[128,1024]{1,0:T(8,128)(2,1)S(1)}, bf16[128,1024]{1,0:T(8,128)(2,1)S(1)}, u32[]{:S(2)}, u32[]{:S(2)}) collective-permute-start(bf16[128,1024]{1,0:T(8,128)(2,1)S(1)} %get-tuple-element.497), channel_id=1, source_target_pairs={{256,0},{260,4},{264,8},{268,12},{272,16},{276,20},{280,24},{284,2... | collective-permute-start | bytes 786440 | tf_op jit(solution)/shard_map/ppermute | solution.py:18
  211.7 21.1 %collective-permute-start.26 = (bf16[128,1024]{1,0:T(8,128)(2,1)S(1)}, bf16[128,1024]{1,0:T(8,128)(2,1)S(1)}, u32[]{:S(2)}, u32[]{:S(2)}) collective-permute-start(bf16[128,1024]{1,0:T(8,128)(2,1)S(1)} %get-tuple-element.498), channel_id=1, source_target_pairs={{128,0},{132,4},{136,8},{140,12},{144,16},{148,20},{152,24},{156,2... | collective-permute-start | bytes 786440 | tf_op jit(solution)/shard_map/ppermute | solution.py:18
  218.8 17.2 %collective-permute-start.25 = (bf16[128,1024]{1,0:T(8,128)(2,1)S(1)}, bf16[128,1024]{1,0:T(8,128)(2,1)S(1)}, u32[]{:S(2)}, u32[]{:S(2)}) collective-permute-start(bf16[128,1024]{1,0:T(8,128)(2,1)S(1)} %get-tuple-element.499), channel_id=1, source_target_pairs={{64,0},{68,4},{72,8},{76,12},{80,16},{84,20},{88,24},{92,28},{96,3... | collective-permute-start | bytes 786440 | tf_op jit(solution)/shard_map/ppermute | solution.py:18
  220.8 260.5 %collective-permute-start.24 = (bf16[128,1024]{1,0:T(8,128)(2,1)S(1)}, bf16[128,1024]{1,0:T(8,128)(2,1)}, u32[]{:S(2)}, u32[]{:S(2)}) collective-permute-start(bf16[128,1024]{1,0:T(8,128)(2,1)S(1)} %get-tuple-element.500), channel_id=1, source_target_pairs={{32,0},{36,4},{40,8},{44,12},{48,16},{52,20},{56,24},{60,28},{64,3... | collective-permute-start | bytes 786440 | tf_op jit(solution)/shard_map/ppermute | solution.py:18
  223.7 269.3 %collective-permute-start.23 = (bf16[128,1024]{1,0:T(8,128)(2,1)S(1)}, bf16[128,1024]{1,0:T(8,128)(2,1)}, u32[]{:S(2)}, u32[]{:S(2)}) collective-permute-start(bf16[128,1024]{1,0:T(8,128)(2,1)S(1)} %get-tuple-element.501), channel_id=1, source_target_pairs={{16,0},{20,4},{24,8},{28,12},{32,16},{36,20},{40,24},{44,28},{48,3... | collective-permute-start | bytes 786440 | tf_op jit(solution)/shard_map/ppermute | solution.py:18
  229.5 298.9 %collective-permute-start.22 = (bf16[128,1024]{1,0:T(8,128)(2,1)S(1)}, bf16[128,1024]{1,0:T(8,128)(2,1)}, u32[]{:S(2)}, u32[]{:S(2)}) collective-permute-start(bf16[128,1024]{1,0:T(8,128)(2,1)S(1)} %get-tuple-element.502), channel_id=1, source_target_pairs={{8,0},{12,4},{16,8},{20,12},{24,16},{28,20},{32,24},{36,28},{40,32... | collective-permute-start | bytes 786440 | tf_op jit(solution)/shard_map/ppermute | solution.py:18
  232.8 297.5 %collective-permute-start.14 = (bf16[128,1024]{1,0:T(8,128)(2,1)}, bf16[128,1024]{1,0:T(8,128)(2,1)}, u32[]{:S(2)}, u32[]{:S(2)}) collective-permute-start(bf16[128,1024]{1,0:T(8,128)(2,1)} %get-tuple-element.503), channel_id=1, source_target_pairs={{4,0},{8,4},{12,8},{16,12},{20,16},{24,20},{28,24},{32,28},{36,32}... | collective-permute-start | bytes 786440 | tf_op jit(solution)/shard_map/ppermute | solution.py:18
  236.0 297.7 %collective-permute-start.20 = (bf16[128,1024]{1,0:T(8,128)(2,1)S(1)}, bf16[128,1024]{1,0:T(8,128)(2,1)}, u32[]{:S(2)}, u32[]{:S(2)}) collective-permute-start(bf16[128,1024]{1,0:T(8,128)(2,1)S(1)} %get-tuple-element.504), channel_id=1, source_target_pairs={{256,0},{260,4},{264,8},{268,12},{272,16},{276,20},{280,24},{284,2... | collective-permute-start | bytes 786440 | tf_op jit(solution)/shard_map/ppermute | solution.py:18
  481.3 61.8 %collective-permute-start.19 = (bf16[128,1024]{1,0:T(8,128)(2,1)S(1)}, bf16[128,1024]{1,0:T(8,128)(2,1)S(1)}, u32[]{:S(2)}, u32[]{:S(2)}) collective-permute-start(bf16[128,1024]{1,0:T(8,128)(2,1)S(1)} %get-tuple-element.505), channel_id=1, source_target_pairs={{128,0},{132,4},{136,8},{140,12},{144,16},{148,20},{152,24},{156,2... | collective-permute-start | bytes 786440 | tf_op jit(solution)/shard_map/ppermute | solution.py:18
  493.0 50.2 %collective-permute-start.18 = (bf16[128,1024]{1,0:T(8,128)(2,1)S(1)}, bf16[128,1024]{1,0:T(8,128)(2,1)S(1)}, u32[]{:S(2)}, u32[]{:S(2)}) collective-permute-start(bf16[128,1024]{1,0:T(8,128)(2,1)S(1)} %get-tuple-element.506), channel_id=1, source_target_pairs={{64,0},{68,4},{72,8},{76,12},{80,16},{84,20},{88,24},{92,28},{96,3... | collective-permute-start | bytes 786440 | tf_op jit(solution)/shard_map/ppermute | solution.py:18
  528.4 15.0 %collective-permute-start.17 = (bf16[128,1024]{1,0:T(8,128)(2,1)S(1)}, bf16[128,1024]{1,0:T(8,128)(2,1)S(1)}, u32[]{:S(2)}, u32[]{:S(2)}) collective-permute-start(bf16[128,1024]{1,0:T(8,128)(2,1)S(1)} %get-tuple-element.507), channel_id=1, source_target_pairs={{32,0},{36,4},{40,8},{44,12},{48,16},{52,20},{56,24},{60,28},{64,3... | collective-permute-start | bytes 786440 | tf_op jit(solution)/shard_map/ppermute | solution.py:18
  530.3 19.4 %collective-permute-start.16 = (bf16[128,1024]{1,0:T(8,128)(2,1)S(1)}, bf16[128,1024]{1,0:T(8,128)(2,1)S(1)}, u32[]{:S(2)}, u32[]{:S(2)}) collective-permute-start(bf16[128,1024]{1,0:T(8,128)(2,1)S(1)} %get-tuple-element.508), channel_id=1, source_target_pairs={{16,0},{20,4},{24,8},{28,12},{32,16},{36,20},{40,24},{44,28},{48,3... | collective-permute-start | bytes 786440 | tf_op jit(solution)/shard_map/ppermute | solution.py:18
  533.7 26.3 %collective-permute-start.15 = (bf16[128,1024]{1,0:T(8,128)(2,1)S(1)}, bf16[128,1024]{1,0:T(8,128)(2,1)S(1)}, u32[]{:S(2)}, u32[]{:S(2)}) collective-permute-start(bf16[128,1024]{1,0:T(8,128)(2,1)S(1)} %get-tuple-element.509), channel_id=1, source_target_pairs={{8,0},{12,4},{16,8},{20,12},{24,16},{28,20},{32,24},{36,28},{40,32... | collective-permute-start | bytes 786440 | tf_op jit(solution)/shard_map/ppermute | solution.py:18
  (6 other events, 33.2 us)
where the time goes:
time: 565 us; the launch traced here: 562 us
  blocking collectives  270 us (48%)
  starting transfers between devices  132 us (23%)
  waiting for transfers between devices  57.2 us (10%)
  matrix products  54.5 us (10%)
  local copies, waits for them, and re-layouts  24.5 us (4%)
  other arithmetic  22.6 us (4%)
    psum x1, blocking collectives, body(): gain_grad = lax.psum(gain_local, 'seq') / math.sqrt(seq_devices * tok_rows)  243 us
    ppermute x28, starting transfers between devices, shifted(): return lax.ppermute(x, axis, pairs)  132 us
    ppermute x28, waiting for transfers between devices, shifted(): return lax.ppermute(x, axis, pairs)  57.2 us
    dot_general x16, matrix products, contract_cols(): lax.dot_general(left_side, right_side, (((1,), (1,)), ((), ())), preferre...  19.9 us
    psum x1, blocking collectives, body(): squares = lax.psum(jnp.sum(context_f * context_f, axis=1), 'head')  18.2 us
    dot_general x8, matrix products, backward_head(): jnp.dot(score_grad, key_head, preferred_element_type=f32).astype(bf16)  14.4 us
  transfers between devices with their start and end apart: 28, of which 7 were waited for; matrix products, arithmetic and copies ran while one was open for 2% of the time, Pallas kernels for 0%

commit v1 on v0

v1 whole, which is shorter than its diff:
```python
import functools
import math

import jax
import jax.numpy as jnp
from jax import lax
from jax.experimental import pallas as pl
from jax.experimental.pallas import tpu as pltpu
from jax.sharding import PartitionSpec as P

D = 4096
HEAD_DIM = 128
EPSILON = 1e-06
MESH = pl.DeviceIdType.MESH
NEG = -1e30
LOG2E = math.log2(math.e)

SLOT = {0: 0, 16: 1, 64: 2, 1: 3, 2: 4, 4: 5, 32: 6, 8: 7}
LEVEL = {1: 0, 2: 1, 4: 2, 8: 3, 16: 4, 32: 5, 64: 6}
STEP_OWN = (0,)
STEPS_FAR = ((16, 64), (1, 2), (4, 32), (8,))
KEYS, VALUES, QUERIES, GRADS, STATS = range(5)
UNROLL = 2


def dot_nt(a, b):
    return lax.dot_general(a, b, (((1,), (1,)), ((), ())), preferred_element_type=jnp.float32)


def dot_nn(a, b):
    return jnp.dot(a, b, preferred_element_type=jnp.float32)


def wide(x, times):
    return x if times == 1 else jnp.concatenate([x] * times, axis=1)


def kernel(
    n_seq,
    n_head,
    heads,
    q_in,
    k_in,
    v_in,
    g_in,
    gain_ref,
    levels_ref,
    normed_ref,
    dq_ref,
    dk_ref,
    dv_ref,
    gain_out,
    kb,
    vb,
    qb,
    gb,
    tb,
    og,
    ctx,
    scores,
    acc,
    mx,
    sm,
    dots,
    dk_acc,
    dv_acc,
    ex,
    gain_acc,
    gain_got,
    send_sem,
    recv_sem,
    local_sem,
    ex_send,
    ex_recv,
    gain_send,
    gain_recv,
):
    f32 = jnp.float32
    bf16 = jnp.bfloat16
    rows = q_in.shape[0]
    dim = HEAD_DIM
    scale = 1.0 / math.sqrt(dim)
    scale2 = scale * LOG2E
    me = lax.axis_index("seq")
    my_head = lax.axis_index("head")
    bufs = {KEYS: kb, VALUES: vb, QUERIES: qb, GRADS: gb, STATS: tb}
    height = {KEYS: rows, VALUES: rows, QUERIES: rows, GRADS: rows, STATS: 2 * heads}
    rounds = len(LEVEL)

    def col(h):
        return pl.ds(pl.multiple_of(h * dim, dim), dim)

    def place(stream):
        return me if stream in (KEYS, VALUES) else n_seq - 1 - me

    def at(stream, spot):
        return spot if stream in (KEYS, VALUES) else n_seq - 1 - spot

    def block(stream, level):
        size = height[stream]
        return bufs[stream].at[pl.ds(SLOT[level] * size, size)]

    def copy(stream, level, source, step):
        target = at(stream, lax.rem(place(stream) + step + n_seq, n_seq))
        return pltpu.make_async_remote_copy(
            src_ref=block(stream, source),
            dst_ref=block(stream, level),
            send_sem=send_sem.at[stream, LEVEL[level]],
            recv_sem=recv_sem.at[stream, LEVEL[level]],
            device_id={"seq": target},
            device_id_type=MESH,
        )

    def edges(stream, level):
        p = place(stream)
        if level == 1:
            even = lax.rem(p, 2) == 0
            return ((0, 1, even), (2, -1, jnp.logical_and(jnp.logical_not(even), p >= 3)))
        source, step = {2: (0, 2), 16: (0, 16), 64: (0, 64), 4: (2, 2), 8: (4, 4), 32: (16, 16)}[level]
        return ((source, step, jnp.logical_and(p >= source, p + step < n_seq)),)

    def send(stream, level, source):
        for origin, step, condition in edges(stream, level):
            if origin == source:
                pl.when(condition)(copy(stream, level, origin, step).start)

    def send_done(stream, level):
        for origin, step, condition in edges(stream, level):
            pl.when(condition)(copy(stream, level, origin, step).wait_send)

    def got(stream, level):
        pl.when(place(stream) >= level)(copy(stream, level, 0, 2).wait_recv)

    loads = [
        pltpu.make_async_copy(k_in, block(KEYS, 0), local_sem.at[0]),
        pltpu.make_async_copy(v_in, block(VALUES, 0), local_sem.at[1]),
        pltpu.make_async_copy(q_in, block(QUERIES, 0), local_sem.at[2]),
        pltpu.make_async_copy(g_in, og, local_sem.at[3]),
    ]
    for load in loads:
        load.start()

    def swap(bit):
        return me + bit - 2 * bit * lax.rem(me // bit, 2)

    barrier = pltpu.get_barrier_semaphore()
    greeted = 0
    for step in (2, n_seq - 2, 4, n_seq - 4, 16, n_seq - 16, 64):
        pl.semaphore_signal(
            barrier, inc=1, device_id={"seq": lax.rem(me + step, n_seq)}, device_id_type=MESH
        )
        greeted += 1
    for bit in (1, 2, 4, 8, 16, 32):
        pl.semaphore_signal(barrier, inc=1, device_id={"seq": swap(bit)}, device_id_type=MESH)
        greeted += 1
    for step in range(1, n_head):
        pl.semaphore_signal(
            barrier, inc=1, device_id={"head": lax.rem(my_head + step, n_head)}, device_id_type=MESH
        )
        greeted += 1

    for stream in (KEYS, VALUES, QUERIES, GRADS, STATS):
        for level in LEVEL:

            @pl.when(place(stream) < level)
            def _(stream=stream, level=level):
                ref = block(stream, level)
                ref[...] = jnp.zeros(ref.shape, ref.dtype)

    for load in loads:
        load.wait()
    pl.semaphore_wait(barrier, greeted)

    for level in (2, 1, 16, 64):
        send(KEYS, level, 0)
        send(VALUES, level, 0)
    for level in (2, 1, 16, 64):
        send(QUERIES, level, 0)

    def bias_of(h, level, stream):
        if level == 0:
            return jnp.float32(0.0)
        live = jnp.logical_and(levels_ref[h, LEVEL[level]] == 1, place(stream) >= level)
        return jnp.where(live, jnp.float32(0.0), jnp.float32(NEG))

    row_id = lax.broadcasted_iota(jnp.int32, (rows, rows), 0)
    col_id = lax.broadcasted_iota(jnp.int32, (rows, rows), 1)

    def each_head(body):
        def some(i, carry):
            for j in range(UNROLL):
                body(i * UNROLL + j)
            return carry

        lax.fori_loop(0, heads // UNROLL, some, 0)

    def forward_step(step):
        first = step == STEP_OWN
        top = SLOT[step[0]] * rows
        count = len(step) * rows

        def one(h):
            q = qb[0:rows, col(h)]
            k = kb[top : top + count, col(h)]
            v = vb[top : top + count, col(h)]
            s = dot_nt(q, k) * scale2
            if first:
                s = jnp.where(col_id <= row_id, s, NEG)
                high = s
            else:
                parts = [
                    s[:, j * rows : (j + 1) * rows] + bias_of(h, level, KEYS)
                    for j, level in enumerate(step)
                ]
                high = functools.reduce(jnp.maximum, parts)
                s = parts[0] if len(parts) == 1 else jnp.concatenate(parts, axis=1)
            scores[h, :, top : top + count] = s
            new = jnp.broadcast_to(jnp.max(high, axis=1, keepdims=True), (rows, dim))
            if not first:
                old = mx[h]
                new = jnp.maximum(old, new)
            p = jnp.exp2(s - wide(new, len(step)))
            total = functools.reduce(
                jnp.add, [p[:, j * rows : (j + 1) * rows] for j in range(len(step))]
            )
            total = jnp.broadcast_to(jnp.sum(total, axis=1, keepdims=True), (rows, dim))
            out = dot_nn(p.astype(bf16), v)
            if first:
                acc[:, col(h)] = out
                sm[h] = total
            else:
                fade = jnp.exp2(old - new)
                acc[:, col(h)] = acc[:, col(h)] * fade + out
                sm[h] = sm[h] * fade + total
            mx[h] = new

        each_head(one)

    forward_step(STEP_OWN)
    for stream in (KEYS, VALUES):
        got(stream, 2)
        send(stream, 4, 2)
        send(stream, 1, 2)
    for stream in (KEYS, VALUES):
        got(stream, 16)
        send(stream, 32, 16)
    got(QUERIES, 2)
    send(QUERIES, 4, 2)
    send(QUERIES, 1, 2)
    got(QUERIES, 16)
    send(QUERIES, 32, 16)
    for stream in (KEYS, VALUES):
        got(stream, 64)
    forward_step((16, 64))
    got(QUERIES, 4)
    send(QUERIES, 8, 4)
    got(KEYS, 1)
    got(VALUES, 1)
    forward_step((1, 2))
    for stream in (KEYS, VALUES):
        got(stream, 4)
        send(stream, 8, 4)
    got(KEYS, 32)
    got(VALUES, 32)
    forward_step((4, 32))
    got(KEYS, 8)
    got(VALUES, 8)
    forward_step((8,))

    def finish(h, carry):
        squares, pulls = carry
        total = sm[h]
        c = (acc[:, col(h)] * (1.0 / total)).astype(bf16)
        ctx[:, col(h)] = c
        c = c.astype(f32)
        lse = mx[h] + jnp.log2(total)
        mx[h] = lse
        tb[pl.ds(h, 1), :] = lse.T[0:1, :]
        pull = gain_ref[0:1, col(h)] * og[:, col(h)].astype(f32) * c
        return squares + c * c, pulls + pull

    zero = jnp.zeros((rows, dim), f32)
    squares, pulls = lax.fori_loop(0, heads, finish, (zero, zero))
    ex[0, 0:1, :] = jnp.sum(squares.T, axis=0, keepdims=True)
    ex[0, 1:2, :] = jnp.sum(pulls.T, axis=0, keepdims=True)
    ex[0, 2:8, :] = jnp.zeros((6, rows), f32)
    swaps = [
        pltpu.make_async_remote_copy(
            src_ref=ex.at[0],
            dst_ref=ex.at[step],
            send_sem=ex_send.at[step],
            recv_sem=ex_recv.at[step],
            device_id={"head": lax.rem(my_head + step, n_head)},
            device_id_type=MESH,
        )
        for step in range(1, n_head)
    ]
    for one in swaps:
        one.start()
    for one in swaps:
        one.wait()
    whole = functools.reduce(jnp.add, [ex[step] for step in range(n_head)])
    inverse_row = lax.rsqrt(whole[0:1, :] / D + EPSILON)
    pull_row = inverse_row * inverse_row * inverse_row * whole[1:2, :] / D
    inverse = jnp.broadcast_to(inverse_row, (dim, rows)).T
    pull_back = jnp.broadcast_to(pull_row, (dim, rows)).T

    def make_grad(h):
        c = ctx[:, col(h)].astype(f32)
        scaled = gain_ref[0:1, col(h)] * og[:, col(h)].astype(f32)
        gb[0:rows, col(h)] = (inverse * scaled - pull_back * c).astype(bf16)

    each_head(make_grad)
    for level in (2, 1, 16, 64):
        send(GRADS, level, 0)

    def make_dots(h):
        c = ctx[:, col(h)].astype(f32)
        both = gb[0:rows, col(h)].astype(f32) * c
        row = jnp.sum(both.T, axis=0, keepdims=True)
        tb[pl.ds(heads + h, 1), :] = row
        dots[h] = jnp.broadcast_to(row, (dim, rows)).T

    each_head(make_dots)
    for level in (2, 1, 16, 64):
        send(STATS, level, 0)

    def make_normed(h):
        c = ctx[:, col(h)].astype(f32) * inverse
        normed_ref[:, col(h)] = (c * gain_ref[0:1, col(h)]).astype(bf16)
        gain_acc[0, 0:1, col(h)] = jnp.sum(og[:, col(h)].astype(f32) * c, axis=0, keepdims=True)

    each_head(make_normed)

    def gain_copy(r):
        return pltpu.make_async_remote_copy(
            src_ref=gain_acc.at[r],
            dst_ref=gain_got.at[r],
            send_sem=gain_send.at[r],
            recv_sem=gain_recv.at[r],
            device_id={"seq": swap(2**r)},
            device_id_type=MESH,
        )

    def gain_next(r):
        gain_copy(r).wait()
        gain_acc[r + 1] = gain_acc[r] + gain_got[r]
        if r + 1 < rounds:
            gain_copy(r + 1).start()

    gain_copy(0).start()

    def query_side(h):
        g = gb[0:rows, col(h)]
        lse = mx[h]
        dot = dots[h]
        total = jnp.zeros((rows, dim), f32)
        for j in range(0, len(SLOT), 2):
            span = slice(j * rows, (j + 2) * rows)
            pull = dot_nt(g, vb[span, col(h)])
            p = jnp.exp2(scores[h, :, span] - wide(lse, 2))
            ds = (p * (pull - wide(dot, 2))).astype(bf16)
            total = total + dot_nn(ds, kb[span, col(h)])
        dq_ref[:, col(h)] = (total * scale).astype(bf16)

    def key_step(step):
        first = step == STEP_OWN
        slot = SLOT[step[0]]
        top = slot * rows
        count = len(step) * rows

        def one(h):
            k = kb[0:rows, col(h)]
            v = vb[0:rows, col(h)]
            q = qb[top : top + count, col(h)]
            g = gb[top : top + count, col(h)]
            shift = []
            dot = []
            for j, level in enumerate(step):
                base = (slot + j) * 2 * heads
                shift.append(bias_of(h, level, QUERIES) - tb[pl.ds(base + h, 1), :])
                dot.append(tb[pl.ds(base + heads + h, 1), :])
            shift = wide(shift[0], 1) if len(step) == 1 else jnp.concatenate(shift, axis=1)
            dot = wide(dot[0], 1) if len(step) == 1 else jnp.concatenate(dot, axis=1)
            s = dot_nt(k, q) * scale2 + shift
            if first:
                s = jnp.where(row_id <= col_id, s, NEG)
            p = jnp.exp2(s)
            pull = dot_nt(v, g)
            ds = (p * (pull - dot)).astype(bf16)
            dv = dot_nn(p.astype(bf16), g)
            dk = dot_nn(ds, q)
            if first:
                dv_acc[:, col(h)] = dv
                dk_acc[:, col(h)] = dk
            elif step == STEPS_FAR[-1]:
                dv_ref[:, col(h)] = (dv_acc[:, col(h)] + dv).astype(bf16)
                dk_ref[:, col(h)] = ((dk_acc[:, col(h)] + dk) * scale).astype(bf16)
            else:
                dv_acc[:, col(h)] += dv
                dk_acc[:, col(h)] += dk

        each_head(one)

    key_step(STEP_OWN)
    gain_next(0)
    for stream in (GRADS, STATS):
        got(stream, 2)
        send(stream, 4, 2)
        send(stream, 1, 2)
    for stream in (GRADS, STATS):
        got(stream, 16)
        send(stream, 32, 16)
    gain_next(1)
    each_head(query_side)
    gain_next(2)
    for stream in (GRADS, STATS):
        got(stream, 4)
        send(stream, 8, 4)
    gain_next(3)
    for stream in (QUERIES, GRADS, STATS):
        got(stream, 64)
    key_step((16, 64))
    gain_next(4)
    for stream in (QUERIES, GRADS, STATS):
        got(stream, 1)
    key_step((1, 2))
    gain_next(5)
    for stream in (QUERIES, GRADS, STATS):
        got(stream, 32)
    key_step((4, 32))
    gain_next(6)
    gain_out[...] = gain_acc[rounds] * (1.0 / math.sqrt(n_seq * rows))
    for stream in (QUERIES, GRADS, STATS):
        got(stream, 8)
    key_step((8,))

    for stream in (KEYS, VALUES, QUERIES, GRADS, STATS):
        for level in LEVEL:
            send_done(stream, level)


def body(queries, key_rows, values, out_grad, norm_gain, head_levels):
    f32 = jnp.float32
    bf16 = jnp.bfloat16
    rows, width = queries.shape
    heads = width // HEAD_DIM
    n_seq = lax.axis_size("seq")
    n_head = lax.axis_size("head")
    slots = len(SLOT)
    rounds = len(LEVEL)
    full = jax.ShapeDtypeStruct((rows, width), bf16)
    anywhere = pl.BlockSpec(memory_space=pl.ANY)
    vmem = pl.BlockSpec(memory_space=pltpu.VMEM)
    smem = pl.BlockSpec(memory_space=pltpu.SMEM)
    normed, dq, dk, dv, gain = pl.pallas_call(
        functools.partial(kernel, n_seq, n_head, heads),
        out_shape=(full, full, full, full, jax.ShapeDtypeStruct((1, width), f32)),
        in_specs=[anywhere] * 4 + [vmem, smem],
        out_specs=[vmem] * 5,
        scratch_shapes=[
            pltpu.VMEM((slots * rows, width), bf16),
            pltpu.VMEM((slots * rows, width), bf16),
            pltpu.VMEM((slots * rows, width), bf16),
            pltpu.VMEM((slots * rows, width), bf16),
            pltpu.VMEM((slots * 2 * heads, rows), f32),
            pltpu.VMEM((rows, width), bf16),
            pltpu.VMEM((rows, width), bf16),
            pltpu.VMEM((heads, rows, slots * rows), f32),
            pltpu.VMEM((rows, width), f32),
            pltpu.VMEM((heads, rows, HEAD_DIM), f32),
            pltpu.VMEM((heads, rows, HEAD_DIM), f32),
            pltpu.VMEM((heads, rows, HEAD_DIM), f32),
            pltpu.VMEM((rows, width), f32),
            pltpu.VMEM((rows, width), f32),
            pltpu.VMEM((n_head, 8, rows), f32),
            pltpu.VMEM((rounds + 1, 1, width), f32),
            pltpu.VMEM((rounds, 1, width), f32),
            pltpu.SemaphoreType.DMA((5, rounds)),
            pltpu.SemaphoreType.DMA((5, rounds)),
            pltpu.SemaphoreType.DMA((4,)),
            pltpu.SemaphoreType.DMA((n_head,)),
            pltpu.SemaphoreType.DMA((n_head,)),
            pltpu.SemaphoreType.DMA((rounds,)),
            pltpu.SemaphoreType.DMA((rounds,)),
        ],
        compiler_params=pltpu.CompilerParams(
            collective_id=0, has_side_effects=True, vmem_limit_bytes=48 * 2**20
        ),
        name="logsparse_layer",
    )(queries, key_rows, values, out_grad, norm_gain.reshape(1, width), head_levels)
    return normed, dq, dk, dv, gain.reshape(width)


def solution(mesh):
    placed = (
        P("seq", "head"),
        P("seq", "head"),
        P("seq", "head"),
        P("seq", "head"),
        P("head"),
        P("head", None),
    )
    return jax.shard_map(
        body,
        mesh=mesh,
        in_specs=placed,
        out_specs=(
            P("seq", "head"),
            P("seq", "head"),
            P("seq", "head"),
            P("seq", "head"),
            P("head"),
        ),
        check_vma=False,
    )
```

time: 565 us -> 142 us (0.25)
  the two profiles are of different devices: /device:TPU:74 before, /device:TPU:32 now
where the time goes in v1:
time: 142 us
  Pallas kernels  132 us (93%)
  local copies, waits for them, and re-layouts  8.57 us (6%)
    pallas_call x1, Pallas kernels, body(): pl.pallas_call(functools.partial(kernel, n_seq, n_head, heads), out_shape...  132 us
    unnamed x17, local copies, waits for them, and re-layouts  8.57 us

profile of v1, /device:TPU:32, one launch (start us, length us, event | category | flops | bytes accessed | tf_op | source)
XLA Modules:
  0.0 141.6 jit_solution(10427904452229615289)
XLA Ops:
  0.6 0.0 copy-start
  0.6 0.9 copy-done
  1.6 0.0 copy-start.1
  1.6 0.9 copy-done.1
  2.5 0.0 copy-start.2
  2.5 0.9 copy-done.2
  3.5 0.0 copy-start.3
  3.5 0.9 copy-done.3
  4.4 0.0 copy-start.4
  4.4 0.7 copy-done.4
  5.1 0.0 copy-start.5
  5.1 0.7 copy-done.5
  5.8 132.4 %logsparse_layer.1 = (bf16[128,1024]{1,0:T(8,128)(2,1)S(1)}, bf16[128,1024]{1,0:T(8,128)(2,1)S(1)}, bf16[128,1024]{1,0:T(8,128)(2,1)S(1)}, bf16[128,1024]{1,0:T(8,128)(2,1)S(1)}, f32[1,1024]{1,0:T(1,128)S(1)}) custom-call(bf16[128,1024]{1,0:T(8,128)(2,1)S(1)} %copy-done, bf16[128,1024]{1,0:T(8,128)(2,1)S(1)} %copy-done.1, bf16[128,1024]{1,0:T(8,128)(2,1)S(1)} %copy-done.2, ...), custom_call_target="tpu_custom_call" | custom-call | tf_op jit(solution)/shard_map/logsparse_layer/pallas_call | solution.py:456
  138.2 0.7 copy.16
  138.9 0.7 copy.17
  139.6 0.7 copy.18
  140.3 0.7 copy.19
  141.0 0.6 copy.20
Async XLA Ops:
  0.6 1.0 copy-start
  1.6 0.9 copy-start.1
  2.5 0.9 copy-start.2
  3.5 0.9 copy-start.3
  4.4 0.7 copy-start.4
  5.1 0.7 copy-start.5

commit v2 on v1

v2 whole, which is shorter than its diff:
```python
import functools
import math

import jax
import jax.numpy as jnp
from jax import lax
from jax.experimental import pallas as pl
from jax.experimental.pallas import tpu as pltpu
from jax.sharding import PartitionSpec as P

D = 4096
HEAD_DIM = 128
EPSILON = 1e-06
MESH = pl.DeviceIdType.MESH
NEG = -1e30
LOG2E = math.log2(math.e)

VIA8, VIA32 = "via8", "via32"
SLOT = {0: 0, 16: 1, 64: 2, 1: 3, 2: 4, 4: 5, 32: 6, 8: 7, VIA8: 8, VIA32: 9}
BLOCKS = 8
LEVEL = {1: 0, 2: 1, 4: 2, 8: 3, 16: 4, 32: 5, 64: 6}
SEM = {**LEVEL, VIA8: 7, VIA32: 8}
RING = 16
STEP_OWN = (0,)
STEPS_FAR = ((16, 64), (1, 2), (4, 32), (8,))
KEYS, VALUES, QUERIES, GRADS, STATS = range(5)
CHUNKS = 4
AROUND = (2, 3)
FORWARD = tuple((array, chunk) for chunk in range(CHUNKS) for array in (KEYS, VALUES))
BACKWARD = tuple((GRADS, chunk) for chunk in range(CHUNKS))
DIRECT = ((QUERIES, 0), (STATS, 0))
STREAMS = FORWARD + BACKWARD + DIRECT
SEMS = {stream: i for i, stream in enumerate(STREAMS)}


def dot_nt(a, b):
    return lax.dot_general(a, b, (((1,), (1,)), ((), ())), preferred_element_type=jnp.float32)


def dot_nn(a, b):
    return jnp.dot(a, b, preferred_element_type=jnp.float32)


def wide(x, times):
    return x if times == 1 else jnp.concatenate([x] * times, axis=1)


def kernel(
    n_seq,
    n_head,
    heads,
    q_in,
    k_in,
    v_in,
    g_in,
    gain_in,
    levels_in,
    normed_ref,
    dq_ref,
    dk_ref,
    dv_ref,
    gain_out,
    kb,
    vb,
    qb,
    gb,
    tb,
    og,
    gain_ref,
    levels_ref,
    ctx,
    scores,
    acc,
    mx,
    sm,
    dots,
    dk_acc,
    dv_acc,
    ex,
    gain_acc,
    gain_got,
    send_sem,
    recv_sem,
    local_sem,
    ex_send,
    ex_recv,
    gain_send,
    gain_recv,
):
    f32 = jnp.float32
    bf16 = jnp.bfloat16
    rows = q_in.shape[0]
    dim = HEAD_DIM
    scale = 1.0 / math.sqrt(dim)
    scale2 = scale * LOG2E
    me = lax.axis_index("seq")
    my_head = lax.axis_index("head")
    part = heads * dim // CHUNKS
    bufs = {KEYS: kb, VALUES: vb, QUERIES: qb, GRADS: gb, STATS: tb}

    def col(h):
        return pl.ds(pl.multiple_of(h * dim, dim), dim)

    def place(stream):
        return me if stream[0] in (KEYS, VALUES) else n_seq - 1 - me

    def at(stream, spot):
        return spot if stream[0] in (KEYS, VALUES) else n_seq - 1 - spot

    def block(stream, level):
        array, chunk = stream
        size = 2 * heads if array == STATS else rows
        span = pl.ds(SLOT[level] * size, size)
        if stream in DIRECT:
            return bufs[array].at[span] if array == STATS else bufs[array].at[:, span]
        return bufs[array].at[chunk, span]

    def copy(stream, level, source, target):
        return pltpu.make_async_remote_copy(
            src_ref=block(stream, source),
            dst_ref=block(stream, level),
            send_sem=send_sem.at[SEMS[stream], SEM[level]],
            recv_sem=recv_sem.at[SEMS[stream], SEM[level]],
            device_id={"seq": at(stream, target)},
            device_id_type=MESH,
        )

    def spot(stream):
        p = place(stream)
        y = lax.rem(p // 2, 8)
        return p, y, lax.rem(p // RING, 4), p - lax.rem(p, RING)

    def in_ring(p, by):
        y = lax.rem(p // 2 + by, 8)
        return p - lax.rem(p, RING) + 2 * y + lax.rem(p, 2)

    def edges(stream, level):
        p, y, x, base = spot(stream)
        if stream in DIRECT:
            return ((0, p + level, p + level < n_seq),) if level in LEVEL else ()
        if level == 1:
            even = lax.rem(p, 2) == 0
            return ((0, p + 1, even), (2, p - 1, jnp.logical_and(jnp.logical_not(even), p >= 3)))
        if level == 2:
            last = y == 7
            return (
                (0, p + 2, jnp.logical_not(last)),
                (16, p - 14, jnp.logical_and(last, p >= 16)),
            )
        if stream[1] in AROUND:
            if level == VIA8:
                low = y < 4
                target = in_ring(p, 7)
                return (
                    (0, target, low),
                    (16, target, jnp.logical_and(jnp.logical_not(low), base >= RING)),
                )
            if level == 8:
                return ((VIA8, in_ring(p, 5), arrives(stream, VIA8)),)
            if level == VIA32:
                return ((0, jnp.where(x == 0, p + 48, p - 16), p + 32 < n_seq),)
            if level == 32:
                return ((VIA32, jnp.where(x == 3, p - 16, p + 48), arrives(stream, VIA32)),)
        elif level in (VIA8, VIA32):
            return ()
        source, step = {16: (0, 16), 64: (0, 64), 4: (2, 2), 8: (4, 4), 32: (16, 16)}[level]
        return ((source, p + step, jnp.logical_and(p >= source, p + step < n_seq)),)

    def arrives(stream, level):
        p, y, x, base = spot(stream)
        if level == VIA8:
            return jnp.logical_or(jnp.logical_or(y <= 2, y == 7), base >= RING)
        if level == VIA32:
            return jnp.where(x == 3, p - 48, p + 16) + 32 < n_seq
        return p >= level

    def send(stream, level, source):
        for origin, target, condition in edges(stream, level):
            if origin == source:
                pl.when(condition)(copy(stream, level, origin, target).start)

    def send_done(stream, level):
        for origin, target, condition in edges(stream, level):
            pl.when(condition)(copy(stream, level, origin, target).wait_send)

    def got(stream, level):
        if level in LEVEL or (stream not in DIRECT and stream[1] in AROUND):
            there = in_ring(place(stream), 1)
            pl.when(arrives(stream, level))(copy(stream, level, 0, there).wait_recv)

    def pass_on(stream, level):
        got(stream, level)
        for onward in SEM:
            send(stream, onward, level)

    loads = [
        pltpu.make_async_copy(source, target, local_sem.at[i])
        for i, (source, target) in enumerate(
            (
                *(
                    (source.at[:, pl.ds(i * part, part)], target.at[i, pl.ds(0, rows)])
                    for source, target in ((k_in, kb), (v_in, vb), (q_in, qb))
                    for i in range(CHUNKS)
                ),
                (g_in, og),
                (gain_in, gain_ref),
                (levels_in, levels_ref),
            )
        )
    ]
    for load in loads:
        load.start()

    my_core, my_y, my_x, my_z = lax.rem(me, 2), lax.rem(me // 2, 8), lax.rem(me // RING, 4), me // (4 * RING)
    groups = (
        (8, my_y, lambda i: me - 2 * my_y + 2 * i),
        (4, 2 * my_z + my_core, lambda i: me + 4 * RING * (i // 2 - my_z) + lax.rem(i, 2) - my_core),
        (4, my_x, lambda i: me + RING * (i - my_x)),
    )

    barrier = pltpu.get_barrier_semaphore()
    greeted = 0
    partners = [lax.rem(me + step, n_seq) for step in (1, 2, 4, 8, 16, 32, 48)]
    partners += [lax.rem(me + n_seq - step, n_seq) for step in (1, 2, 4, 8, 16, 32, 48, 64)]
    partners.append(me + 1 - 2 * my_core)
    partners += [in_ring(me, by) for by in (1, 3, 5, 7)]
    for size, mine, member in groups:
        partners += [member(lax.rem(mine + i, size)) for i in range(1, size)]
    for partner in partners:
        pl.semaphore_signal(barrier, inc=1, device_id={"seq": partner}, device_id_type=MESH)
        greeted += 1
    for step in range(1, n_head):
        pl.semaphore_signal(
            barrier, inc=1, device_id={"head": lax.rem(my_head + step, n_head)}, device_id_type=MESH
        )
        greeted += 1

    for array in bufs:
        size = 2 * heads if array == STATS else rows
        for level in LEVEL:

            @pl.when(place((array, 0)) < level)
            def _(ref=bufs[array], span=pl.ds(SLOT[level] * size, size)):
                if array == STATS:
                    ref[span, :] = jnp.zeros((size, ref.shape[1]), ref.dtype)
                else:
                    for i in range(CHUNKS):
                        ref[i, span, :] = jnp.zeros((size, part), ref.dtype)

    for load in loads:
        load.wait()
    pl.semaphore_wait(barrier, greeted)

    own_order = (16, 64, 2, VIA8, VIA32, 1)
    for level in own_order:
        for stream in FORWARD:
            send(stream, level, 0)

    def bias_of(h, level, stream):
        if level == 0:
            return jnp.float32(0.0)
        live = jnp.logical_and(levels_ref[h, LEVEL[level]] == 1, place(stream) >= level)
        return jnp.where(live, jnp.float32(0.0), jnp.float32(NEG))

    row_id = lax.broadcasted_iota(jnp.int32, (rows, rows), 0)
    col_id = lax.broadcasted_iota(jnp.int32, (rows, rows), 1)

    per_chunk = heads // CHUNKS

    def each_head(body):
        def some(i, carry):
            for j in range(per_chunk):
                body(i * per_chunk + j, lambda ref, span: ref[i, span, j * dim : (j + 1) * dim])
            return carry

        lax.fori_loop(0, CHUNKS, some, 0)

    def forward_step(step):
        first = step == STEP_OWN
        top = SLOT[step[0]] * rows
        count = len(step) * rows

        def one(h, of):
            q = of(qb, slice(0, rows))
            k = of(kb, slice(top, top + count))
            v = of(vb, slice(top, top + count))
            s = dot_nt(q, k) * scale2
            if first:
                s = jnp.where(col_id <= row_id, s, NEG)
                high = s
            else:
                parts = [
                    s[:, j * rows : (j + 1) * rows] + bias_of(h, level, (KEYS, 0))
                    for j, level in enumerate(step)
                ]
                high = functools.reduce(jnp.maximum, parts)
                s = parts[0] if len(parts) == 1 else jnp.concatenate(parts, axis=1)
            scores[h, :, top : top + count] = s
            new = jnp.broadcast_to(jnp.max(high, axis=1, keepdims=True), (rows, dim))
            if not first:
                old = mx[h]
                new = jnp.maximum(old, new)
            p = jnp.exp2(s - wide(new, len(step)))
            total = functools.reduce(
                jnp.add, [p[:, j * rows : (j + 1) * rows] for j in range(len(step))]
            )
            total = jnp.broadcast_to(jnp.sum(total, axis=1, keepdims=True), (rows, dim))
            out = dot_nn(p.astype(bf16), v)
            if first:
                acc[:, col(h)] = out
                sm[h] = total
            else:
                fade = jnp.exp2(old - new)
                acc[:, col(h)] = acc[:, col(h)] * fade + out
                sm[h] = sm[h] * fade + total
            mx[h] = new

        each_head(one)

    forward_step(STEP_OWN)
    for stream in FORWARD:
        for level in (16, 2, VIA8, VIA32):
            pass_on(stream, level)
    for stream in FORWARD:
        got(stream, 64)
    forward_step((16, 64))
    for stream in FORWARD:
        pass_on(stream, 4)
    for level in (8, 4, 2, 1, 32, 16, 64):
        send((QUERIES, 0), level, 0)
    for stream in FORWARD:
        got(stream, 1)
    forward_step((1, 2))
    for stream in FORWARD:
        got(stream, 32)
    forward_step((4, 32))
    for stream in FORWARD:
        got(stream, 8)
    forward_step((8,))

    def finish(h, carry):
        squares, pulls = carry
        total = sm[h]
        c = (acc[:, col(h)] * (1.0 / total)).astype(bf16)
        ctx[:, col(h)] = c
        c = c.astype(f32)
        lse = mx[h] + jnp.log2(total)
        mx[h] = lse
        tb[pl.ds(h, 1), :] = lse.T[0:1, :]
        pull = gain_ref[0:1, col(h)] * og[:, col(h)].astype(f32) * c
        return squares + c * c, pulls + pull

    zero = jnp.zeros((rows, dim), f32)
    squares, pulls = lax.fori_loop(0, heads, finish, (zero, zero))
    ex[0, 0:1, :] = jnp.sum(squares.T, axis=0, keepdims=True)
    ex[0, 1:2, :] = jnp.sum(pulls.T, axis=0, keepdims=True)
    ex[0, 2:8, :] = jnp.zeros((6, rows), f32)
    swaps = [
        pltpu.make_async_remote_copy(
            src_ref=ex.at[0],
            dst_ref=ex.at[step],
            send_sem=ex_send.at[step],
            recv_sem=ex_recv.at[step],
            device_id={"head": lax.rem(my_head + step, n_head)},
            device_id_type=MESH,
        )
        for step in range(1, n_head)
    ]
    for one in swaps:
        one.start()
    for one in swaps:
        one.wait()
    whole = functools.reduce(jnp.add, [ex[step] for step in range(n_head)])
    inverse_row = lax.rsqrt(whole[0:1, :] / D + EPSILON)
    pull_row = inverse_row * inverse_row * inverse_row * whole[1:2, :] / D
    inverse = jnp.broadcast_to(inverse_row, (dim, rows)).T
    pull_back = jnp.broadcast_to(pull_row, (dim, rows)).T

    def make_grad(chunk, j):
        h = chunk * per_chunk + j
        c = ctx[:, col(h)].astype(f32)
        scaled = gain_ref[0:1, col(h)] * og[:, col(h)].astype(f32)
        gb[chunk, 0:rows, j * dim : (j + 1) * dim] = (inverse * scaled - pull_back * c).astype(bf16)

    for stream in BACKWARD:
        for i in range(per_chunk):
            make_grad(stream[1], i)
        for level in own_order:
            send(stream, level, 0)

    def make_dots(h, of):
        c = ctx[:, col(h)].astype(f32)
        both = of(gb, slice(0, rows)).astype(f32) * c
        row = jnp.sum(both.T, axis=0, keepdims=True)
        tb[pl.ds(heads + h, 1), :] = row
        dots[h] = jnp.broadcast_to(row, (dim, rows)).T

    each_head(make_dots)
    for level in (8, 4, 2, 1, 32, 16, 64):
        send((STATS, 0), level, 0)

    def make_normed(h, of):
        c = ctx[:, col(h)].astype(f32) * inverse
        normed_ref[:, col(h)] = (c * gain_ref[0:1, col(h)]).astype(bf16)
        gain_acc[0:1, col(h)] = jnp.sum(og[:, col(h)].astype(f32) * c, axis=0, keepdims=True)

    each_head(make_normed)

    def gain_copies(r):
        size, mine, member = groups[r]
        first = sum(group[0] for group in groups[:r])
        return first, [
            pltpu.make_async_remote_copy(
                src_ref=gain_acc,
                dst_ref=gain_got.at[first + mine],
                send_sem=gain_send.at[first + i],
                recv_sem=gain_recv.at[first + i],
                device_id={"seq": member(lax.rem(mine + i, size))},
                device_id_type=MESH,
            )
            for i in range(1, size)
        ]

    def gain_start(r):
        first, copies = gain_copies(r)
        for one in copies:
            one.start()
        gain_got[first + groups[r][1]] = gain_acc[...]

    def gain_end(r):
        first, copies = gain_copies(r)
        for one in copies:
            one.wait()
        gain_acc[...] = functools.reduce(
            jnp.add, [gain_got[first + i] for i in range(groups[r][0])]
        )

    gain_start(0)

    def query_side(h, of):
        g = of(gb, slice(0, rows))
        lse = mx[h]
        dot = dots[h]
        total = jnp.zeros((rows, dim), f32)
        for j in range(0, BLOCKS, 2):
            span = slice(j * rows, (j + 2) * rows)
            pull = dot_nt(g, of(vb, span))
            p = jnp.exp2(scores[h, :, span] - wide(lse, 2))
            ds = (p * (pull - wide(dot, 2))).astype(bf16)
            total = total + dot_nn(ds, of(kb, span))
        dq_ref[:, col(h)] = (total * scale).astype(bf16)

    def key_step(step):
        first = step == STEP_OWN
        slot = SLOT[step[0]]
        top = slot * rows
        count = len(step) * rows

        def one(h, of):
            k = of(kb, slice(0, rows))
            v = of(vb, slice(0, rows))
            q = of(qb, slice(top, top + count))
            g = of(gb, slice(top, top + count))
            shift = []
            dot = []
            for j, level in enumerate(step):
                base = (slot + j) * 2 * heads
                shift.append(bias_of(h, level, (QUERIES, 0)) - tb[pl.ds(base + h, 1), :])
                dot.append(tb[pl.ds(base + heads + h, 1), :])
            shift = wide(shift[0], 1) if len(step) == 1 else jnp.concatenate(shift, axis=1)
            dot = wide(dot[0], 1) if len(step) == 1 else jnp.concatenate(dot, axis=1)
            s = dot_nt(k, q) * scale2 + shift
            if first:
                s = jnp.where(row_id <= col_id, s, NEG)
            p = jnp.exp2(s)
            pull = dot_nt(v, g)
            ds = (p * (pull - dot)).astype(bf16)
            dv = dot_nn(p.astype(bf16), g)
            dk = dot_nn(ds, q)
            if first:
                dv_acc[:, col(h)] = dv
                dk_acc[:, col(h)] = dk
            elif step == STEPS_FAR[-1]:
                dv_ref[:, col(h)] = (dv_acc[:, col(h)] + dv).astype(bf16)
                dk_ref[:, col(h)] = ((dk_acc[:, col(h)] + dk) * scale).astype(bf16)
            else:
                dv_acc[:, col(h)] += dv
                dk_acc[:, col(h)] += dk

        each_head(one)

    def key_got(level):
        for stream in BACKWARD + DIRECT:
            got(stream, level)

    for stream in BACKWARD:
        for level in (16, 2, VIA8, VIA32):
            pass_on(stream, level)
    key_step(STEP_OWN)
    gain_end(0)
    gain_start(1)
    for stream in BACKWARD:
        pass_on(stream, 4)
    each_head(query_side)
    gain_end(1)
    gain_start(2)
    for stream in DIRECT:
        for level in (16, 2, 4):
            got(stream, level)
    key_got(64)
    key_step((16, 64))
    key_got(1)
    key_step((1, 2))
    gain_end(2)
    gain_out[...] = gain_acc[...] * (1.0 / math.sqrt(n_seq * rows))
    key_got(32)
    key_step((4, 32))
    key_got(8)
    key_step((8,))

    for stream in STREAMS:
        for level in SEM:
            send_done(stream, level)


def body(queries, key_rows, values, out_grad, norm_gain, head_levels):
    f32 = jnp.float32
    bf16 = jnp.bfloat16
    rows, width = queries.shape
    heads = width // HEAD_DIM
    n_seq = lax.axis_size("seq")
    n_head = lax.axis_size("head")
    slots = BLOCKS
    stops = len(SLOT)
    full = jax.ShapeDtypeStruct((rows, width), bf16)
    hbm = pl.BlockSpec(memory_space=pltpu.HBM)
    vmem = pl.BlockSpec(memory_space=pltpu.VMEM)
    normed, dq, dk, dv, gain = pl.pallas_call(
        functools.partial(kernel, n_seq, n_head, heads),
        out_shape=(full, full, full, full, jax.ShapeDtypeStruct((1, width), f32)),
        in_specs=[hbm] * 6,
        out_specs=[vmem] * 5,
        scratch_shapes=[
            pltpu.VMEM((CHUNKS, stops * rows, width // CHUNKS), bf16),
            pltpu.VMEM((CHUNKS, stops * rows, width // CHUNKS), bf16),
            pltpu.VMEM((CHUNKS, slots * rows, width // CHUNKS), bf16),
            pltpu.VMEM((CHUNKS, stops * rows, width // CHUNKS), bf16),
            pltpu.VMEM((slots * 2 * heads, rows), f32),
            pltpu.VMEM((rows, width), bf16),
            pltpu.VMEM((1, width), f32),
            pltpu.SMEM(head_levels.shape, jnp.int32),
            pltpu.VMEM((rows, width), bf16),
            pltpu.VMEM((heads, rows, slots * rows), f32),
            pltpu.VMEM((rows, width), f32),
            pltpu.VMEM((heads, rows, HEAD_DIM), f32),
            pltpu.VMEM((heads, rows, HEAD_DIM), f32),
            pltpu.VMEM((heads, rows, HEAD_DIM), f32),
            pltpu.VMEM((rows, width), f32),
            pltpu.VMEM((rows, width), f32),
            pltpu.VMEM((n_head, 8, rows), f32),
            pltpu.VMEM((1, width), f32),
            pltpu.VMEM((16, 1, width), f32),
            pltpu.SemaphoreType.DMA((len(STREAMS), len(SEM))),
            pltpu.SemaphoreType.DMA((len(STREAMS), len(SEM))),
            pltpu.SemaphoreType.DMA((3 * CHUNKS + 3,)),
            pltpu.SemaphoreType.DMA((n_head,)),
            pltpu.SemaphoreType.DMA((n_head,)),
            pltpu.SemaphoreType.DMA((16,)),
            pltpu.SemaphoreType.DMA((16,)),
        ],
        compiler_params=pltpu.CompilerParams(
            collective_id=0, has_side_effects=True, vmem_limit_bytes=60 * 2**20
        ),
        name="logsparse_layer",
    )(queries, key_rows, values, out_grad, norm_gain.reshape(1, width), head_levels)
    return normed, dq, dk, dv, gain.reshape(width)


def solution(mesh):
    placed = (
        P("seq", "head"),
        P("seq", "head"),
        P("seq", "head"),
        P("seq", "head"),
        P("head"),
        P("head", None),
    )
    return jax.shard_map(
        body,
        mesh=mesh,
        in_specs=placed,
        out_specs=(
            P("seq", "head"),
            P("seq", "head"),
            P("seq", "head"),
            P("seq", "head"),
            P("head"),
        ),
        check_vma=False,
    )
```

time: 142 us -> 122 us (0.86)
  the two profiles are of different devices: /device:TPU:32 before, /device:TPU:418 now
where the time goes in v2:
time: 122 us; the launch traced here: 121 us
  Pallas kernels  116 us (95%)
  local copies, waits for them, and re-layouts  5.1 us (4%)
    pallas_call x1, Pallas kernels, body(): pl.pallas_call(functools.partial(kernel, n_seq, n_head, heads), out_shape...  116 us
    unnamed x13, local copies, waits for them, and re-layouts  5.1 us

profile of v2, /device:TPU:418, one launch (start us, length us, event | category | flops | bytes accessed | tf_op | source)
XLA Modules:
  0.0 121.3 jit_solution(10011922454347019262)
XLA Ops:
  0.6 115.6 %logsparse_layer.1 = (bf16[128,1024]{1,0:T(8,128)(2,1)}, bf16[128,1024]{1,0:T(8,128)(2,1)}, bf16[128,1024]{1,0:T(8,128)(2,1)}, bf16[128,1024]{1,0:T(8,128)(2,1)}, f32[1,1024]{1,0:T(1,128)}) custom-call(bf16[128,1024]{1,0:T(8,128)(2,1)} %q_in.1, bf16[128,1024]{1,0:T(8,128)(2,1)} %k_in.1, bf16[128,1024]{1,0:T(8,128)(2,1)} %v_in.1, bf16[128,1024]{1,0:T(8,128)(2,1)} %g_in.1, ...), custom_call_target="tpu_custom_call" | custom-call | tf_op jit(solution)/shard_map/logsparse_layer/pallas_call | solution.py:538
  116.2 0.0 copy-start.2
  116.2 1.7 %copy.16 = bf16[128,1024]{1,0:T(8,128)(2,1)} copy(bf16[128,1024]{1,0:T(8,128)(2,1)} %get-tuple-element.20) | data formatting | bytes 524288
  117.9 0.0 copy-done.2
  117.9 0.0 copy-start.1
  117.9 0.7 copy.17
  118.6 0.3 copy-done.1
  119.0 0.0 copy-start
  119.0 0.7 copy.18
  119.7 0.3 copy-done
  120.0 0.0 copy-start.3
  120.0 0.7 copy.19
  120.7 0.0 copy-done.3
  120.7 0.6 copy.20
Async XLA Ops:
  116.2 1.7 %copy-start.2 = (bf16[128,1024]{1,0:T(8,128)(2,1)S(1)}, bf16[128,1024]{1,0:T(8,128)(2,1)}, u32[]{:S(2)}) copy-start(bf16[128,1024]{1,0:T(8,128)(2,1)} %get-tuple-element.21) | copy-start | bytes 786436
  117.9 1.0 copy-start.1
  119.0 1.0 copy-start
  120.0 0.7 copy-start.3

commit v3 on v2

--- a/solution.py
+++ b/solution.py
@@ -25,11 +25,12 @@
 STEPS_FAR = ((16, 64), (1, 2), (4, 32), (8,))
 KEYS, VALUES, QUERIES, GRADS, STATS = range(5)
 CHUNKS = 4
-AROUND = (2, 3)
-FORWARD = tuple((array, chunk) for chunk in range(CHUNKS) for array in (KEYS, VALUES))
+FORWARD = tuple((array, chunk) for chunk in range(CHUNKS) for array in (KEYS, VALUES, QUERIES))
 BACKWARD = tuple((GRADS, chunk) for chunk in range(CHUNKS))
-DIRECT = ((QUERIES, 0), (STATS, 0))
+DIRECT = ((STATS, 0),)
 STREAMS = FORWARD + BACKWARD + DIRECT
+AROUND8 = ((KEYS, 3), (VALUES, 3), (GRADS, 2), (GRADS, 3))
+AROUND32 = ((KEYS, 2), (VALUES, 2), (KEYS, 3), (VALUES, 3), (GRADS, 2), (GRADS, 3))
 SEMS = {stream: i for i, stream in enumerate(STREAMS)}
 
 
@@ -147,21 +148,20 @@
                 (0, p + 2, jnp.logical_not(last)),
                 (16, p - 14, jnp.logical_and(last, p >= 16)),
             )
-        if stream[1] in AROUND:
-            if level == VIA8:
-                low = y < 4
-                target = in_ring(p, 7)
-                return (
-                    (0, target, low),
-                    (16, target, jnp.logical_and(jnp.logical_not(low), base >= RING)),
-                )
+        if level in (VIA8, 8) and stream in AROUND8:
             if level == 8:
                 return ((VIA8, in_ring(p, 5), arrives(stream, VIA8)),)
-            if level == VIA32:
-                return ((0, jnp.where(x == 0, p + 48, p - 16), p + 32 < n_seq),)
+            low = y < 4
+            target = in_ring(p, 7)
+            return (
+                (0, target, low),
+                (16, target, jnp.logical_and(jnp.logical_not(low), base >= RING)),
+            )
+        if level in (VIA32, 32) and stream in AROUND32:
             if level == 32:
                 return ((VIA32, jnp.where(x == 3, p - 16, p + 48), arrives(stream, VIA32)),)
-        elif level in (VIA8, VIA32):
+            return ((0, jnp.where(x == 0, p + 48, p - 16), p + 32 < n_seq),)
+        if level not in LEVEL:
             return ()
         source, step = {16: (0, 16), 64: (0, 64), 4: (2, 2), 8: (4, 4), 32: (16, 16)}[level]
         return ((source, p + step, jnp.logical_and(p >= source, p + step < n_seq)),)
@@ -184,7 +184,7 @@
             pl.when(condition)(copy(stream, level, origin, target).wait_send)
 
     def got(stream, level):
-        if level in LEVEL or (stream not in DIRECT and stream[1] in AROUND):
+        if edges(stream, level):
             there = in_ring(place(stream), 1)
             pl.when(arrives(stream, level))(copy(stream, level, 0, there).wait_recv)
 
@@ -220,10 +220,7 @@
 
     barrier = pltpu.get_barrier_semaphore()
     greeted = 0
-    partners = [lax.rem(me + step, n_seq) for step in (1, 2, 4, 8, 16, 32, 48)]
-    partners += [lax.rem(me + n_seq - step, n_seq) for step in (1, 2, 4, 8, 16, 32, 48, 64)]
-    partners.append(me + 1 - 2 * my_core)
-    partners += [in_ring(me, by) for by in (1, 3, 5, 7)]
+    partners = [lax.rem(me + step, n_seq) for step in (1, 2, 4, 8, 16, 32, 48, 64, 80, 112, 124, 126)]
     for size, mine, member in groups:
         partners += [member(lax.rem(mine + i, size)) for i in range(1, size)]
     for partner in partners:
@@ -252,9 +249,11 @@
     pl.semaphore_wait(barrier, greeted)
 
     own_order = (16, 64, 2, VIA8, VIA32, 1)
-    for level in own_order:
-        for stream in FORWARD:
-            send(stream, level, 0)
+    for arrays in ((KEYS, VALUES), (QUERIES,)):
+        for level in own_order:
+            for stream in FORWARD:
+                if stream[0] in arrays:
+                    send(stream, level, 0)
 
     def bias_of(h, level, stream):
         if level == 0:
@@ -317,25 +316,33 @@
 
         each_head(one)
 
+    def forward_got(level):
+        for stream in FORWARD:
+            if stream[0] != QUERIES:
+                got(stream, level)
+
     forward_step(STEP_OWN)
-    for stream in FORWARD:
-        for level in (16, 2, VIA8, VIA32):
-            pass_on(stream, level)
-    for stream in FORWARD:
-        got(stream, 64)
+    ordered = sorted(FORWARD, key=lambda stream: stream[0] == QUERIES)
+    for stream in ordered:
+        if stream[0] != QUERIES:
+            for level in (16, 2, VIA8, VIA32):
+                pass_on(stream, level)
+    for stream in ordered:
+        if stream[0] == QUERIES:
+            pass_on(stream, 16)
+            pass_on(stream, 2)
+        else:
+            pass_on(stream, 4)
+    forward_got(64)
     forward_step((16, 64))
-    for stream in FORWARD:
-        pass_on(stream, 4)
-    for level in (8, 4, 2, 1, 32, 16, 64):
-        send((QUERIES, 0), level, 0)
-    for stream in FORWARD:
-        got(stream, 1)
+    for stream in ordered:
+        if stream[0] == QUERIES:
+            pass_on(stream, 4)
+    forward_got(1)
     forward_step((1, 2))
-    for stream in FORWARD:
-        got(stream, 32)
+    forward_got(32)
     forward_step((4, 32))
-    for stream in FORWARD:
-        got(stream, 8)
+    forward_got(8)
     forward_step((8,))
 
     def finish(h, carry):
@@ -404,8 +411,6 @@
         normed_ref[:, col(h)] = (c * gain_ref[0:1, col(h)]).astype(bf16)
         gain_acc[0:1, col(h)] = jnp.sum(og[:, col(h)].astype(f32) * c, axis=0, keepdims=True)
 
-    each_head(make_normed)
-
     def gain_copies(r):
         size, mine, member = groups[r]
         first = sum(group[0] for group in groups[:r])
@@ -434,8 +439,6 @@
         gain_acc[...] = functools.reduce(
             jnp.add, [gain_got[first + i] for i in range(groups[r][0])]
         )
-
-    gain_start(0)
 
     def query_side(h, of):
         g = of(gb, slice(0, rows))
@@ -492,7 +495,12 @@
     def key_got(level):
         for stream in BACKWARD + DIRECT:
             got(stream, level)
-
+        for stream in FORWARD:
+            if stream[0] == QUERIES:
+                got(stream, level)
+
+    each_head(make_normed)
+    gain_start(0)
     for stream in BACKWARD:
         for level in (16, 2, VIA8, VIA32):
             pass_on(stream, level)
@@ -523,6 +531,11 @@
             send_done(stream, level)
 
 
+def hand_over(*refs):
+    for source, target in zip(refs[:5], refs[5:]):
+        target[...] = source[...]
+
+
 def body(queries, key_rows, values, out_grad, norm_gain, head_levels):
     f32 = jnp.float32
     bf16 = jnp.bfloat16
@@ -535,7 +548,7 @@
     full = jax.ShapeDtypeStruct((rows, width), bf16)
     hbm = pl.BlockSpec(memory_space=pltpu.HBM)
     vmem = pl.BlockSpec(memory_space=pltpu.VMEM)
-    normed, dq, dk, dv, gain = pl.pallas_call(
+    results = pl.pallas_call(
         functools.partial(kernel, n_seq, n_head, heads),
         out_shape=(full, full, full, full, jax.ShapeDtypeStruct((1, width), f32)),
         in_specs=[hbm] * 6,
@@ -573,6 +586,13 @@
         ),
         name="logsparse_layer",
     )(queries, key_rows, values, out_grad, norm_gain.reshape(1, width), head_levels)
+    normed, dq, dk, dv, gain = pl.pallas_call(
+        hand_over,
+        out_shape=(full, full, full, full, jax.ShapeDtypeStruct((1, width), f32)),
+        in_specs=[vmem] * 5,
+        out_specs=[vmem] * 5,
+        name="hand_over",
+    )(*results)
     return normed, dq, dk, dv, gain.reshape(width)
 
 

time: 122 us -> 113 us (0.926)
  the two profiles are of different devices: /device:TPU:418 before, /device:TPU:16 now
where the time goes in v3:
time: 113 us; the launch traced here: 112 us
  Pallas kernels  112 us (99%)
    pallas_call x1, Pallas kernels, body(): pl.pallas_call(functools.partial(kernel, n_seq, n_head, heads), out_shape...  110 us

profile of v3, /device:TPU:16, one launch (start us, length us, event | category | flops | bytes accessed | tf_op | source)
XLA Modules:
  0.0 112.4 jit_solution(1661942053136965448)
XLA Ops:
  0.6 109.6 %logsparse_layer.1 = (bf16[128,1024]{1,0:T(8,128)(2,1)}, bf16[128,1024]{1,0:T(8,128)(2,1)}, bf16[128,1024]{1,0:T(8,128)(2,1)}, bf16[128,1024]{1,0:T(8,128)(2,1)}, f32[1,1024]{1,0:T(1,128)}) custom-call(bf16[128,1024]{1,0:T(8,128)(2,1)} %q_in.1, bf16[128,1024]{1,0:T(8,128)(2,1)} %k_in.1, bf16[128,1024]{1,0:T(8,128)(2,1)} %v_in.1, bf16[128,1024]{1,0:T(8,128)(2,1)} %g_in.1, ...), custom_call_target="tpu_custom_call" | custom-call | tf_op jit(solution)/shard_map/logsparse_layer/pallas_call | solution.py:551
  110.2 2.2 %hand_over.1 = (bf16[128,1024]{1,0:T(8,128)(2,1)}, bf16[128,1024]{1,0:T(8,128)(2,1)}, bf16[128,1024]{1,0:T(8,128)(2,1)}, bf16[128,1024]{1,0:T(8,128)(2,1)}, f32[1,1024]{1,0:T(1,128)}) custom-call(bf16[128,1024]{1,0:T(8,128)(2,1)} %get-tuple-element.15.refs_0_, bf16[128,1024]{1,0:T(8,128)(2,1)} %get-tuple-element.16.refs_1_, ...), custom_call_target="tpu_custom_call" | custom-call | tf_op jit(solution)/shard_map/hand_over/pallas_call | solution.py:589
